TPU v7x, 128 devices: a whole 4x4x4 slice. The times are simulated.
128 devices in a mesh: group: 4 (over x_lo, core), tensor: 32 (over x_hi, y, z).
Axes of the slice: x: 4 (x_hi: 2, x_lo: 2; x = x_hi * 2 + x_lo), y: 4, z: 4, core: 2. Of those that a mesh axis runs over, the one named last changes fastest.
Arguments:
- tokens: bfloat16 [512, 3, 8192], P(('group', 'tensor')), may hold values from -6 to 6
- norm_gain: float32 [8192], replicated, may hold values from 0.25 to 1.75
- w_qkv: bfloat16 [8192, 10240], P(None, 'tensor'), may hold values from -0.0625 to 0.0625
- w_out: bfloat16 [8192, 8192], P('tensor'), may hold values from -0.0625 to 0.0625
- lengths: int32 [128, 4], P(('group', 'tensor')), may hold values from 1 to 512, 1024 in all within a row
- migrate: int32 [128, 4], P(('group', 'tensor')), may hold values from 0 to 3, as said below
- page_order: int32 [128, 12], P(('group', 'tensor')), may hold values from 0 to 11, each once within a row
- kv_pool: bfloat16 [128, 12, 2, 8, 128, 128], P(('group', 'tensor')), as said below
Outputs:
- mixed: bfloat16 [512, 3, 8192], P(('group', 'tensor'))
Inputs may be any that keep to these rules, and one draw needn't show every extreme that they name: `migrate`: on each device every group number is named by exactly 1 row. The 4 lengths of one device sum to 1024. `kv_pool`: cached keys and values of order one or more.
All inputs are finite; a program needn't handle non-finite values.
Results may differ from a plain program's by a relative error of at most 0.013.
Values may be sent and summed in bfloat16 or wider, within the bound.
A program may use at most 128 MiB of HBM per device.

v0:
```python
import jax
import jax.numpy as jnp
from jax import lax
from jax.sharding import Mesh
from jax.sharding import PartitionSpec as P

HEADS = 64
KV_HEADS = 8
HEAD_DIM = 128
PAGE = 128
MAX_PAGES = 4
GROUP = ("group_0", "group_1")
GROUP_TENSOR = ("group_0", "group_1", "tensor")
EPS = 1e-05
ROPE_BASE = 500000.0
NEG_FILL = -1e30


def cut_along(shard, dim, devices):
    lengths = shard.shape
    parts = shard.reshape(*lengths[:dim], devices, lengths[dim] // devices, *lengths[dim + 1 :])
    return jnp.moveaxis(parts, dim, 0)


def joined_along(parts, dim):
    parts = jnp.moveaxis(parts, 0, dim)
    lengths = parts.shape
    return parts.reshape(*lengths[:dim], lengths[dim] * lengths[dim + 1], *lengths[dim + 2 :])


def moved_by_axis(parts, axes, sequence):
    inside = parts.shape[1:]
    out = parts.reshape(*(lax.axis_size(a) for a in axes), *inside)
    for k in sequence:
        out = lax.all_to_all(out, axes[k], k, k, tiled=True)
    return out.reshape(-1, *inside)


def stepwise_exchange(shard, axes, sequence, split_dim, concat_dim):
    parts = cut_along(shard, split_dim, lax.axis_size(axes))
    return joined_along(moved_by_axis(parts, axes, sequence), concat_dim)


def side_by_side(arrays, axis, split_dim, concat_dim, along):
    columns = [a.reshape(*a.shape[:along], -1) for a in arrays]
    both = jnp.concatenate(columns, axis=along)
    out, at, gathered = (
        lax.all_to_all(both, axis, split_axis=split_dim, concat_axis=concat_dim, tiled=True),
        0,
        [],
    )
    for a, column in zip(arrays, columns):
        piece = out[..., at : at + column.shape[along]]
        gathered.append(piece.reshape(*piece.shape[:along], *a.shape[along:]))
        at += column.shape[along]
    return tuple(gathered)


def summed_on_arrival(shard, axis, dim):
    parts = cut_along(shard, dim, lax.axis_size(axis))
    arrived = lax.all_to_all(parts, axis, split_axis=0, concat_axis=0, tiled=True)
    return arrived.astype(jnp.float32).sum(axis=0)


def rotate(values, positions):
    half_dim = values.shape[-1] // 2
    inverse = ROPE_BASE ** (-(jnp.arange(half_dim, dtype=jnp.float32) * 2.0 / values.shape[-1]))
    angles = positions.astype(jnp.float32)[..., None] * inverse
    cosine = jnp.cos(angles)[..., None, :]
    sine = jnp.sin(angles)[..., None, :]
    lower_half = values[..., :half_dim]
    upper_half = values[..., half_dim:]
    return jnp.concatenate(
        [lower_half * cosine - upper_half * sine, upper_half * cosine + lower_half * sine], axis=-1
    )


def cache_stats(queries, pages, row_lens):
    row_total, steps_here, head_count, head_dim = queries.shape
    page_count = pages.shape[1]
    kv_heads = pages.shape[3]
    page_len = pages.shape[4]
    grouped = queries.reshape(row_total, steps_here, kv_heads, head_count // kv_heads, head_dim)
    scores = jnp.einsum(
        "rskgd,rbktd->rskgbt", grouped, pages[:, :, 0], preferred_element_type=jnp.float32
    ) * head_dim ** (-0.5)
    places = (
        jnp.arange(page_count, dtype=jnp.int32)[:, None] * page_len
        + jnp.arange(page_len, dtype=jnp.int32)[None, :]
    )
    inside = (places[None] < row_lens[:, None, None])[:, None, None, None]
    page_top = jnp.max(jnp.where(inside, scores, NEG_FILL), axis=-1)
    weights = jnp.where(inside, jnp.exp(scores - page_top[..., None]), 0.0).astype(jnp.bfloat16)
    page_total = jnp.sum(weights.astype(jnp.float32), axis=-1)
    page_acc = jnp.einsum(
        "rskgbt,rbktd->rskgbd", weights, pages[:, :, 1], preferred_element_type=jnp.float32
    )
    top_score = jnp.max(page_top, axis=-1)
    page_scale = jnp.exp(page_top - top_score[..., None])
    return (
        top_score,
        jnp.sum(page_scale * page_total, axis=-1),
        jnp.sum(page_scale[..., None] * page_acc, axis=-2),
    )


def finish(queries, cache_parts, all_keys, all_values):
    row_total, steps_here, head_count, head_dim = queries.shape
    kv_heads = all_keys.shape[2]
    grouped = queries.reshape(row_total, steps_here, kv_heads, head_count // kv_heads, head_dim)
    scores = jnp.einsum(
        "rskgd,rukd->rskgu", grouped, all_keys, preferred_element_type=jnp.float32
    ) * head_dim ** (-0.5)
    allowed = jnp.arange(all_keys.shape[1])[None, :] <= jnp.arange(steps_here)[:, None]
    allowed = allowed[None, :, None, None, :]
    new_top = jnp.max(jnp.where(allowed, scores, NEG_FILL), axis=-1)
    weights = jnp.where(allowed, jnp.exp(scores - new_top[..., None]), 0.0).astype(jnp.bfloat16)
    new_total = jnp.sum(weights.astype(jnp.float32), axis=-1)
    new_acc = jnp.einsum(
        "rskgu,rukd->rskgd", weights, all_values, preferred_element_type=jnp.float32
    )
    cache_top, cache_total, cache_acc = cache_parts
    top_score = jnp.maximum(cache_top, new_top)
    cache_scale = jnp.exp(cache_top - top_score)
    new_scale = jnp.exp(new_top - top_score)
    merged = (cache_scale[..., None] * cache_acc + new_scale[..., None] * new_acc) / (
        cache_scale * cache_total + new_scale * new_total
    )[..., None]
    return merged.reshape(row_total, steps_here, head_count * head_dim).astype(jnp.bfloat16)


def per_device(tokens, norm_gain, w_qkv, w_out, lengths, migrate, page_order, kv_pool):
    row_lens = lengths[0]
    destinations = migrate[0]
    pool_order = page_order[0]
    page_pool = kv_pool[0]
    row_total = row_lens.shape[0]
    pool_size = page_pool.shape[0]
    slot_ids = jnp.arange(row_total, dtype=jnp.int32)
    sort_keys = destinations * row_total + slot_ids
    row_ranks = jnp.sum((sort_keys[None, :] < sort_keys[:, None]).astype(jnp.int32), axis=1)
    placing = row_ranks[:, None] == slot_ids[None, :]
    pages_used = (row_lens + PAGE - 1) // PAGE
    offsets = jnp.cumsum(pages_used) - pages_used
    sorted_lens = jnp.sum(jnp.where(placing, row_lens[:, None], 0), axis=0)
    sorted_first = jnp.sum(jnp.where(placing, offsets[:, None], 0), axis=0)
    page_slots = jnp.clip(
        sorted_first[:, None] + jnp.arange(MAX_PAGES, dtype=jnp.int32)[None, :], 0, pool_size - 1
    )
    home_pages = page_pool[pool_order[page_slots]]
    new_lens = stepwise_exchange(sorted_lens, GROUP, (0, 1), 0, 0)
    width_q = HEADS * HEAD_DIM
    width_k = KV_HEADS * HEAD_DIM
    keys_so_far = jnp.zeros((row_total, 0, KV_HEADS, HEAD_DIM), jnp.bfloat16)
    values_so_far = jnp.zeros((row_total, 0, KV_HEADS, HEAD_DIM), jnp.bfloat16)
    steps_here = tokens.shape[1]
    floats = tokens.astype(jnp.float32)
    normed = (
        floats * lax.rsqrt(jnp.mean(floats * floats, axis=-1, keepdims=True) + EPS) * norm_gain
    ).astype(jnp.bfloat16)

    def columns(row_piece, row_start):
        return jnp.einsum(
            "rsd,dc->rsc", row_piece, w_qkv, preferred_element_type=jnp.float32
        ).astype(jnp.bfloat16)

    gathered = columns(lax.all_gather(normed, "tensor", axis=0, tiled=True), jnp.int32(0))
    full_rows = lax.all_to_all(gathered, "tensor", split_axis=0, concat_axis=2, tiled=True)
    positions = new_lens[:, None] + 0 + jnp.arange(steps_here, dtype=jnp.int32)[None, :]
    queries = rotate(
        full_rows[..., :width_q]
        .reshape(row_total, steps_here, HEADS, HEAD_DIM)
        .astype(jnp.float32),
        positions,
    ).astype(jnp.bfloat16)
    keys_here = rotate(
        full_rows[..., width_q : width_q + width_k]
        .reshape(row_total, steps_here, KV_HEADS, HEAD_DIM)
        .astype(jnp.float32),
        positions,
    ).astype(jnp.bfloat16)
    values_here = full_rows[..., width_q + width_k :].reshape(
        row_total, steps_here, KV_HEADS, HEAD_DIM
    )
    all_keys = jnp.concatenate([keys_so_far, keys_here], axis=1)
    all_values = jnp.concatenate([values_so_far, values_here], axis=1)
    home_queries = lax.all_to_all(queries, GROUP, split_axis=0, concat_axis=0, tiled=True)
    home_parts = cache_stats(home_queries, home_pages, sorted_lens)
    attended = finish(
        queries,
        tuple(
            (
                part.astype(jnp.float32)
                for part in side_by_side(
                    (
                        home_parts[0].astype(jnp.bfloat16),
                        home_parts[1].astype(jnp.bfloat16),
                        home_parts[2].astype(jnp.bfloat16),
                    ),
                    GROUP,
                    0,
                    0,
                    4,
                )
            )
        ),
        all_keys,
        all_values,
    )
    spread = lax.all_to_all(attended, "tensor", split_axis=2, concat_axis=0, tiled=True)
    summed = summed_on_arrival(
        jnp.einsum("rsc,cd->rsd", spread, w_out, preferred_element_type=jnp.float32).astype(
            jnp.bfloat16
        ),
        "tensor",
        0,
    )
    output = (floats + summed).astype(jnp.bfloat16)
    return output


def solution(mesh):
    split = Mesh(mesh.devices.reshape(2, 2, mesh.shape["tensor"]), ("group_0", "group_1", "tensor"))
    placed = (
        P(GROUP_TENSOR, None, None),
        P(),
        P(None, "tensor"),
        P("tensor", None),
        P(GROUP_TENSOR, None),
        P(GROUP_TENSOR, None),
        P(GROUP_TENSOR, None),
        P(GROUP_TENSOR, None, None, None, None, None),
    )
    return jax.shard_map(
        per_device,
        mesh=split,
        in_specs=placed,
        out_specs=P(GROUP_TENSOR, None, None),
        check_vma=False,
    )
```

profile of v0, /device:TPU:0, one launch (start us, length us, event | category | flops | bytes accessed | tf_op | source)
XLA Modules:
  0.0 344.3 jit_solution(6098262649707031891)
XLA Ops:
  6.5 1.1 fusion.23
  7.7 1.1 fusion.25
  8.8 0.9 copy.227
  9.7 0.7 and_select_fusion.1
  10.5 0.7 bitcast_add_fusion
  11.2 0.7 add_bitcast_fusion
  12.0 0.7 bitcast_subtract_fusion.1
  12.7 0.7 select_reduce_fusion.2
  13.5 0.6 reshape_reshape.3
  14.1 3.2 all-to-all-start.1
  17.5 0.7 gather_fusion
  18.3 7.7 %gather_fusion.1 = bf16[16,2,8,128,128]{4,3,2,1,0:T(8,128)(2,1)} fusion(bf16[12,2,8,128,128]{4,3,2,1,0:T(8,128)(2,1)} %bitcast.155, s32[1024]{0:T(1024)S(1)} %pad_clamp_fusion), kind=kCustom, calls=%fused_computation.1 | custom fusion | bytes 16777280 | tf_op jit(solution)/shard_map/gather | solution.py:150
  26.2 6.0 %fusion.46 = (bf16[4,4,1,8,128,128]{5,4,3,2,1,0:T(8,128)(2,1)}, bf16[4,4,1,8,128,128]{5,4,3,2,1,0:T(8,128)(2,1)}) fusion(bf16[4,4,2,8,128,128]{5,4,3,2,1,0:T(8,128)(2,1)} %bitcast.152), kind=kLoop, calls=%fused_computation.107 | loop fusion | bytes 16777216 | tf_op jit(solution)/shard_map/slice | solution.py:85
  32.3 3.6 %all_to_all.61 = s32[2,2,1]{0,2,1:T(1,128)S(1)} all-to-all(s32[2,2,1]{0,2,1:T(1,128)S(1)} %copy.233), channel_id=1, replica_groups=mesh['group_0'=2,'group_1'=2,'tensor'=32] {'group_1'}, dimensions={1} | all-to-all | bytes 32 | tf_op jit(solution)/shard_map/all_to_all | solution.py:35
  36.1 80.8 %all-gather.2.cloned.1.call-done = bf16[128,3,8192]{2,1,0:T(4,128)(2,1)} async-done(((bf16[4,3,8192]{2,1,0:T(4,128)(2,1)}), bf16[128,3,8192]{2,1,0:T(4,128)(2,1)}) %all-gather.2.cloned.1.call-update) | async-done | bytes 6291472 | tf_op jit(solution)/shard_map/all_gather | solution.py:167
  116.9 12.4 %fusion.16 = bf16[128,3,320]{0,2,1:T(8,128)(2,1)S(1)} fusion(bf16[8192,320]{0,1:T(8,128)(2,1)} %param.10, bf16[128,3,8192]{2,1,0:T(4,128)(2,1)} %all-gather.2.cloned.1.call-done), kind=kOutput, calls=%fused_computation.27 | convolution fusion | flops 2013388800 | bytes 11780096 | tf_op jit(solution)/shard_map/rsd,dc->rsc/dot_general | solution.py:163
  129.3 1.0 copy.229
  130.2 5.9 %all-to-all-start = ((bf16[128,3,320]{2,1,0:T(4,128)(2,1)}), bf16[128,3,320]{2,1,0:T(4,128)(2,1)S(1)}, u32[]{:S(2)}, u32[]{:S(2)}) async-start(bf16[128,3,320]{2,1,0:T(4,128)(2,1)} %copy.229), calls=%async_computation | async-start | bytes 786432 | tf_op jit(solution)/shard_map/all_to_all | solution.py:168
  136.4 11.0 %all-to-all-done = bf16[128,3,320]{2,1,0:T(4,128)(2,1)S(1)} async-done(((bf16[128,3,320]{2,1,0:T(4,128)(2,1)}), bf16[128,3,320]{2,1,0:T(4,128)(2,1)S(1)}, u32[]{:S(2)}, u32[]{:S(2)}) %all-to-all-start) | async-done | bytes 245792 | tf_op jit(solution)/shard_map/all_to_all | solution.py:168
  147.4 0.4 all_to_all.44
  148.0 0.3 reshape.287
  148.6 0.7 copy.237
  149.3 3.4 all-to-all-start.3
  152.7 5.2 %all-to-all-done.3 = bf16[4,3,64,128]{3,2,1,0:T(8,128)(2,1)S(1)} async-done(((bf16[4,3,64,128]{3,2,1,0:T(8,128)(2,1)}), bf16[4,3,64,128]{3,2,1,0:T(8,128)(2,1)S(1)}, u32[]{:S(2)}, u32[]{:S(2)}) %all-to-all-start.3) | async-done | bytes 196640 | tf_op jit(solution)/shard_map/all_to_all | solution.py:187
  158.0 3.6 %fusion.10 = (f32[4,3,8,8,4]{3,1,4,2,0:T(4,128)S(1)}, f32[4,8,4,128,3,8]{3,5,4,2,1,0:T(8,128)S(1)}) fusion(pred[4,4,128]{2,1,0:T(4,128)(4,1)S(1)} %broadcast_compare_fusion, bf16[4,4,1,8,128,128]{5,4,3,2,1,0:T(8,128)(2,1)} %get-tuple-element.11, bf16[4,3,64,128]{3,2,1,0:T(8,128)(2,1)S(1)} %all-to-all-done.3), kind=kOutput, calls=%fused_computation.20 | convolution fusion | flops 101839872 | bytes 5978112 | tf_op jit(solution)/shard_map/rskgd,rbktd->rskgbt/dot_general | solution.py:84
  161.5 1.2 convert_reduce_fusion.1
  162.9 0.7 copy.242
  163.6 0.7 copy.243
  164.2 3.5 %fusion.6 = bf16[4,3,8,8,128]{4,3,1,2,0:T(8,128)(2,1)S(1)} fusion(bf16[4,4,1,8,128,128]{5,4,3,2,1,0:T(8,128)(2,1)} %get-tuple-element.12, f32[4,3,8,8,4]{3,1,4,2,0:T(4,128)S(1)} %get-tuple-element.10, f32[4,8,4,128,3,8]{3,5,4,2,1,0:T(8,128)S(1)} %get-tuple-element.29, f32[4,3,8,8,4]{3,1,4,2,0:T(4,128)S(1)} %get-tuple-element.28, ...), kind=kOutput, calls=%fused_computation.13 | convolution fusion | flops 102531072 | bytes 5990400 | tf_op jit(solution)/shard_map/rskgbt,rbktd->rskgbd/dot_general | solution.py:95
  167.8 1.1 pad_maximum_fusion
  168.9 3.5 %all-to-all-start.4 = ((bf16[4,3,8,8,130]{4,3,2,1,0:T(8,128)(2,1)}), bf16[4,3,8,8,130]{4,3,2,1,0:T(8,128)(2,1)S(1)}, u32[]{:S(2)}, u32[]{:S(2)}) async-start(bf16[4,3,8,8,130]{4,3,2,1,0:T(8,128)(2,1)} %pad_maximum_fusion), calls=%async_computation.4 | async-start | bytes 786432 | tf_op jit(solution)/shard_map/all_to_all | solution.py:48
  172.3 0.8 select_reduce_fusion
  173.2 0.2 convert_reduce_fusion.2
  173.4 6.3 %all-to-all-done.4 = bf16[4,3,8,8,130]{4,3,2,1,0:T(8,128)(2,1)S(1)} async-done(((bf16[4,3,8,8,130]{4,3,2,1,0:T(8,128)(2,1)}), bf16[4,3,8,8,130]{4,3,2,1,0:T(8,128)(2,1)S(1)}, u32[]{:S(2)}, u32[]{:S(2)}) %all-to-all-start.4) | async-done | bytes 199712 | tf_op jit(solution)/shard_map/all_to_all | solution.py:48
  179.9 0.6 copy.291
  180.5 0.6 copy.295
  181.3 0.6 fusion.21
  181.9 6.5 %copy.286 = bf16[4,3,8,8,128]{0,1,4,3,2:T(4,128)(2,1)} copy(bf16[4,3,8,8,128]{4,3,1,2,0:T(8,128)(2,1)S(1)} %fusion.21) | data formatting | bytes 393216 | tf_op jit(solution)/shard_map/convert_element_type | solution.py:129
  188.4 12.6 %reshape.315 = bf16[32,2,1536]{2,1,0:T(2,128)(2,1)S(1)} reshape(bf16[8192,3,4]{2,1,0:T(4,128)(2,1)} %bitcast.153) | data formatting | bytes 393216
  201.0 14.2 %all_to_all.62 = bf16[32,2,1536]{2,1,0:T(2,128)(2,1)S(1)} all-to-all(bf16[32,2,1536]{2,1,0:T(2,128)(2,1)S(1)} %reshape.315), channel_id=1, replica_groups=mesh['group_0'=2,'group_1'=2,'tensor'=32] {'tensor'}, dimensions={0} | all-to-all | bytes 393216 | tf_op jit(solution)/shard_map/all_to_all | solution.py:210
  215.1 10.4 %reshape.316 = bf16[8192,3,4]{2,1,0:T(4,128)(2,1)} reshape(bf16[32,2,1536]{2,1,0:T(2,128)(2,1)S(1)} %all_to_all.62) | data formatting | bytes 393216
  225.5 7.9 %copy.287 = bf16[4,3,32,256]{3,2,0,1:T(8,128)(2,1)S(1)} copy(bf16[4,3,32,256]{0,1,3,2:T(4,128)(2,1)} %bitcast.154) | data formatting | bytes 393216 | tf_op jit(solution)/shard_map/all_to_all | solution.py:210
  233.6 6.7 %convolution_convert_fusion = bf16[128,3,8192]{2,0,1:T(8,128)(2,1)} fusion(bf16[128,3,256]{2,0,1:T(8,128)(2,1)S(1)} %all_to_all.52, bf16[256,8192]{1,0:T(8,128)(2,1)} %param.11), kind=kOutput, calls=%fused_computation.3 | convolution fusion | flops 1613758464 | bytes 10682368 | tf_op jit(solution)/shard_map/rsc,cd->rsd/dot_general | solution.py:212
  240.3 10.2 %reshape.286 = bf16[32,4,3,8192]{3,1,0,2:T(4,128)(2,1)} reshape(bf16[128,3,8192]{2,0,1:T(8,128)(2,1)} %convolution_convert_fusion) | data formatting | bytes 12582912 | tf_op jit(solution)/shard_map/reshape | solution.py:21
  250.4 5.7 %copy.267 = bf16[32,4,3,8192]{3,1,2,0:T(4,128)(2,1)S(1)} copy(bf16[32,4,3,8192]{3,1,0,2:T(4,128)(2,1)} %reshape.286) | data formatting | bytes 12582912 | tf_op jit(solution)/shard_map/reshape | solution.py:21
  256.1 77.5 %all_to_all.63 = bf16[32,4,3,8192]{3,1,2,0:T(4,128)(2,1)S(1)} all-to-all(bf16[32,4,3,8192]{3,1,2,0:T(4,128)(2,1)S(1)} %copy.267), channel_id=1, replica_groups=mesh['group_0'=2,'group_1'=2,'tensor'=32] {'tensor'}, dimensions={0} | all-to-all | bytes 12582912 | tf_op jit(solution)/shard_map/all_to_all | solution.py:61
  333.6 3.0 convert_reduce_fusion
  336.6 0.8 fusion.26
  (50 shorter events, 2.7 us)
Async XLA Ops:
  6.5 10.9 %copy-start = (s32[1,12]{1,0:T(1,128)S(1)}, s32[1,12]{1,0:T(1,128)}, u32[]{:S(2)}) copy-start(s32[1,12]{1,0:T(1,128)} %param.14) | copy-start | bytes 148
  6.5 110.4 %all-gather.2.cloned.1.call-start = ((), (), s32[]{:S(2)}) async-start(), calls=%async_computation.7 | async-start | bytes 8650752 | tf_op jit(solution)/shard_map/all_gather | solution.py:167
  14.1 18.1 %all-to-all-start.1 = ((s32[2,2,1]{1,2,0:T(1,128)}), s32[2,2,1]{1,2,0:T(1,128)S(1)}, u32[]{:S(2)}, u32[]{:S(2)}) async-start(s32[2,2,1]{1,2,0:T(1,128)} %bitcast.15), calls=%async_computation.1 | async-start | bytes 2048 | tf_op jit(solution)/shard_map/all_to_all | solution.py:35
  130.2 17.1 %all-to-all-start = ((bf16[128,3,320]{2,1,0:T(4,128)(2,1)}), bf16[128,3,320]{2,1,0:T(4,128)(2,1)S(1)}, u32[]{:S(2)}, u32[]{:S(2)}) async-start(bf16[128,3,320]{2,1,0:T(4,128)(2,1)} %copy.229), calls=%async_computation | async-start | bytes 786432 | tf_op jit(solution)/shard_map/all_to_all | solution.py:168
  149.3 8.7 %all-to-all-start.3 = ((bf16[4,3,64,128]{3,2,1,0:T(8,128)(2,1)}), bf16[4,3,64,128]{3,2,1,0:T(8,128)(2,1)S(1)}, u32[]{:S(2)}, u32[]{:S(2)}) async-start(bf16[4,3,64,128]{3,2,1,0:T(8,128)(2,1)} %copy.237), calls=%async_computation.3 | async-start | bytes 393216 | tf_op jit(solution)/shard_map/all_to_all | solution.py:187
  168.9 10.9 %all-to-all-start.4 = ((bf16[4,3,8,8,130]{4,3,2,1,0:T(8,128)(2,1)}), bf16[4,3,8,8,130]{4,3,2,1,0:T(8,128)(2,1)S(1)}, u32[]{:S(2)}, u32[]{:S(2)}) async-start(bf16[4,3,8,8,130]{4,3,2,1,0:T(8,128)(2,1)} %pad_maximum_fusion), calls=%async_computation.4 | async-start | bytes 786432 | tf_op jit(solution)/shard_map/all_to_all | solution.py:48
  256.1 81.3 %copy-start.1 = (s32[1,12]{1,0:T(1,128)S(1)}, s32[1,12]{1,0:T(1,128)}, u32[]{:S(2)}) copy-start(s32[1,12]{1,0:T(1,128)} %param.14) | copy-start | bytes 148
  333.6 3.0 copy-start.2
Sparse Core Ops, SparseCore 0:
  10.5 106.3 all-gather.1
where the time goes:
time: 346 us; the launch traced here: 344 us
  waiting for transfers between devices  103 us (30%)
  blocking collectives  95.3 us (28%)
  local copies, waits for them, and re-layouts  75.1 us (22%)
  matrix products  27.6 us (8%)
  starting transfers between devices  16 us (5%)
  between operations  13.7 us (4%)
  other arithmetic  13.5 us (4%)
    all_gather x1, waiting for transfers between devices, per_device(): lax.all_gather(normed, 'tensor', axis=0, tiled=True)  80.8 us
    all_to_all x1, blocking collectives, summed_on_arrival(): lax.all_to_all(parts, axis, split_axis=0, concat_axis=0, tiled=True)  77.5 us
    unnamed x10, local copies, waits for them, and re-layouts  24.2 us
    reshape x2, local copies, waits for them, and re-layouts, cut_along(): shard.reshape(*lengths[:dim], devices, lengths[dim] // devices, *lengths[...  15.8 us
    all_to_all x1, blocking collectives, per_device(): lax.all_to_all(attended, 'tensor', split_axis=2, concat_axis=0, tiled=True)  14.2 us
    dot_general x1, matrix products, columns(): jnp.einsum('rsd,dc->rsc', row_piece, w_qkv, preferred_element_type=jnp.fl...  12.4 us
    all_to_all x1, waiting for transfers between devices, per_device(): lax.all_to_all(gathered, 'tensor', split_axis=0, concat_axis=2, tiled=True)  11 us
    gather x3, local copies, waits for them, and re-layouts, per_device(): home_pages = page_pool[pool_order[page_slots]]  8.41 us
  transfers between devices with their start and end apart: 5, of which 4 were waited for; matrix products, arithmetic and copies ran while one was open for 6% of the time, Pallas kernels for 0%

commit v1 on v0

--- a/solution.py
+++ b/solution.py
@@ -164,7 +164,12 @@
             "rsd,dc->rsc", row_piece, w_qkv, preferred_element_type=jnp.float32
         ).astype(jnp.bfloat16)
 
-    gathered = columns(lax.all_gather(normed, "tensor", axis=0, tiled=True), jnp.int32(0))
+    gathered = columns(
+        jnp.concatenate(
+            lax.all_to_all(jnp.stack([normed] * lax.axis_size("tensor")), "tensor", 0, 0), axis=0
+        ),
+        jnp.int32(0),
+    )
     full_rows = lax.all_to_all(gathered, "tensor", split_axis=0, concat_axis=2, tiled=True)
     positions = new_lens[:, None] + 0 + jnp.arange(steps_here, dtype=jnp.int32)[None, :]
     queries = rotate(

time: 346 us -> 361 us (1.043)
  local copies, waits for them, and re-layouts: 75.1 us -> 100 us
  between operations: 13.7 us -> 0.29 us
  starting transfers between devices: 16 us -> 27.6 us
  matrix products: 27.6 us -> 22.4 us
    all_gather x1 -> x0, waiting for transfers between devices: 80.8 us -> none  [per_device(): lax.all_gather(normed, 'tensor', axis=0, tiled=True)]
    all_to_all x0 -> x1, waiting for transfers between devices: none -> 75.5 us  [per_device(): lax.all_to_all(jnp.stack([normed] * lax.axis_size('tensor')), 'tensor', 0...]
    all_to_all x0 -> x1, starting transfers between devices: none -> 11 us  [per_device(): lax.all_to_all(jnp.stack([normed] * lax.axis_size('tensor')), 'tensor', 0...]
    all_to_all x0 -> x1, local copies, waits for them, and re-layouts: none -> 10.7 us  [per_device(): lax.all_to_all(jnp.stack([normed] * lax.axis_size('tensor')), 'tensor', 0...]
    reshape x0 -> x1, local copies, waits for them, and re-layouts: none -> 9.72 us  [per_device(): jnp.concatenate(lax.all_to_all(jnp.stack([normed] * lax.axis_size('tensor...]
    another operation x0 -> x1, local copies, waits for them, and re-layouts: none -> 5.66 us  [per_device(): jnp.stack([normed] * lax.axis_size('tensor'))]
    dot_general x1, matrix products: 12.4 us -> 7.19 us  [columns(): jnp.einsum('rsd,dc->rsc', row_piece, w_qkv, preferred_element_type=jnp.fl...]
  transfers between devices with their start and end apart: 5 -> 5, of which waited for: 4 -> 5; matrix products, arithmetic and copies ran while one was open for 6% -> 5% of each run, Pallas kernels for 0% -> 0%
where the time goes in v1:
time: 361 us; the launch traced here: 359 us
  local copies, waits for them, and re-layouts  100 us (28%)
  waiting for transfers between devices  99.6 us (28%)
  blocking collectives  95.7 us (27%)
  starting transfers between devices  27.6 us (8%)
  matrix products  22.4 us (6%)
  other arithmetic  13.5 us (4%)
    all_to_all x1, blocking collectives, summed_on_arrival(): lax.all_to_all(parts, axis, split_axis=0, concat_axis=0, tiled=True)  77.5 us
    all_to_all x1, waiting for transfers between devices, per_device(): lax.all_to_all(jnp.stack([normed] * lax.axis_size('tensor')), 'tensor', 0...  75.5 us
    unnamed x10, local copies, waits for them, and re-layouts  24.2 us
    reshape x2, local copies, waits for them, and re-layouts, cut_along(): shard.reshape(*lengths[:dim], devices, lengths[dim] // devices, *lengths[...  15.8 us
    all_to_all x1, blocking collectives, per_device(): lax.all_to_all(attended, 'tensor', split_axis=2, concat_axis=0, tiled=True)  14.6 us
    all_to_all x1, waiting for transfers between devices, per_device(): lax.all_to_all(gathered, 'tensor', split_axis=0, concat_axis=2, tiled=True)  11.3 us
    all_to_all x1, starting transfers between devices, per_device(): lax.all_to_all(jnp.stack([normed] * lax.axis_size('tensor')), 'tensor', 0...  11 us
    all_to_all x1, local copies, waits for them, and re-layouts, per_device(): lax.all_to_all(jnp.stack([normed] * lax.axis_size('tensor')), 'tensor', 0...  10.7 us
  transfers between devices with their start and end apart: 5, of which 5 were waited for; matrix products, arithmetic and copies ran while one was open for 5% of the time, Pallas kernels for 0%

profile of v1, /device:TPU:0, one launch (start us, length us, event | category | flops | bytes accessed | tf_op | source)
XLA Modules:
  0.0 359.3 jit_solution(10977588115887875432)
XLA Ops:
  0.0 0.7 bitcast_add_fusion
  0.7 0.7 add_bitcast_fusion
  1.3 0.7 and_select_fusion.1
  2.2 0.7 bitcast_subtract_fusion.1
  3.0 0.7 select_reduce_fusion.2
  3.8 0.6 reshape_reshape.3
  4.4 3.2 all-to-all-start.2
  7.6 1.1 fusion.20
  8.8 1.1 fusion.22
  9.9 1.4 all-to-all-done.2
  11.4 3.6 %all_to_all.66 = s32[2,2,1]{0,2,1:T(1,128)S(1)} all-to-all(s32[2,2,1]{0,2,1:T(1,128)S(1)} %copy.187), channel_id=1, replica_groups=mesh['group_0'=2,'group_1'=2,'tensor'=32] {'group_1'}, dimensions={1} | all-to-all | bytes 32 | tf_op jit(solution)/shard_map/all_to_all | solution.py:35
  15.0 5.7 %stack.2 = bf16[32,4,3,8192]{3,1,2,0:T(4,128)(2,1)} broadcast(bf16[4,3,8192]{2,0,1:T(4,128)(2,1)S(1)} %fusion.22), dimensions={1,2,3} | broadcast | bytes 6488064 | tf_op jit(solution)/shard_map/stack | solution.py:169
  20.7 11.0 %all-to-all-start = ((bf16[32,4,3,8192]{3,1,2,0:T(4,128)(2,1)}), bf16[32,4,3,8192]{3,1,2,0:T(4,128)(2,1)}, u32[]{:S(2)}, u32[]{:S(2)}) async-start(bf16[32,4,3,8192]{3,1,2,0:T(4,128)(2,1)} %stack.2), calls=%async_computation | async-start | bytes 12582912 | tf_op jit(solution)/shard_map/all_to_all | solution.py:169
  31.8 0.7 gather_fusion
  32.7 7.6 %gather_fusion.1 = bf16[16,2,8,128,128]{4,3,2,1,0:T(8,128)(2,1)} fusion(bf16[12,2,8,128,128]{4,3,2,1,0:T(8,128)(2,1)} %bitcast.158, s32[1024]{0:T(1024)S(1)} %pad_clamp_fusion), kind=kCustom, calls=%fused_computation.1 | custom fusion | bytes 16777280 | tf_op jit(solution)/shard_map/gather | solution.py:150
  40.4 6.1 %fusion.43 = (bf16[4,4,1,8,128,128]{5,4,3,2,1,0:T(8,128)(2,1)}, bf16[4,4,1,8,128,128]{5,4,3,2,1,0:T(8,128)(2,1)}) fusion(bf16[4,4,2,8,128,128]{5,4,3,2,1,0:T(8,128)(2,1)} %bitcast.155), kind=kLoop, calls=%fused_computation.106 | loop fusion | bytes 16777216 | tf_op jit(solution)/shard_map/slice | solution.py:85
  46.7 75.5 %all-to-all-done = bf16[32,4,3,8192]{3,1,2,0:T(4,128)(2,1)} async-done(((bf16[32,4,3,8192]{3,1,2,0:T(4,128)(2,1)}), bf16[32,4,3,8192]{3,1,2,0:T(4,128)(2,1)}, u32[]{:S(2)}, u32[]{:S(2)}) %all-to-all-start) | async-done | bytes 6291488 | tf_op jit(solution)/shard_map/all_to_all | solution.py:169
  122.2 10.7 %copy.182 = bf16[32,4,3,8192]{3,1,0,2:T(4,128)(2,1)} copy(bf16[32,4,3,8192]{3,1,2,0:T(4,128)(2,1)} %all-to-all-done) | data formatting | bytes 12582912 | tf_op jit(solution)/shard_map/all_to_all | solution.py:169
  132.9 9.7 %reshape.289 = bf16[128,3,8192]{2,0,1:T(8,128)(2,1)} reshape(bf16[32,4,3,8192]{3,1,0,2:T(4,128)(2,1)} %copy.182) | data formatting | bytes 12582912 | tf_op jit(solution)/shard_map/reshape | solution.py:168
  142.7 7.2 %fusion.15 = bf16[128,3,320]{0,2,1:T(8,128)(2,1)S(1)} fusion(bf16[128,3,8192]{2,0,1:T(8,128)(2,1)} %reshape.289, bf16[8192,320]{0,1:T(8,128)(2,1)} %param.10), kind=kOutput, calls=%fused_computation.26 | convolution fusion | flops 2013388800 | bytes 11780096 | tf_op jit(solution)/shard_map/rsd,dc->rsc/dot_general | solution.py:163
  149.8 1.0 copy.183
  150.8 6.4 %all-to-all-start.1 = ((bf16[128,3,320]{2,1,0:T(4,128)(2,1)}), bf16[128,3,320]{2,1,0:T(4,128)(2,1)S(1)}, u32[]{:S(2)}, u32[]{:S(2)}) async-start(bf16[128,3,320]{2,1,0:T(4,128)(2,1)} %copy.183), calls=%async_computation.1 | async-start | bytes 786432 | tf_op jit(solution)/shard_map/all_to_all | solution.py:173
  157.4 11.3 %all-to-all-done.1 = bf16[128,3,320]{2,1,0:T(4,128)(2,1)S(1)} async-done(((bf16[128,3,320]{2,1,0:T(4,128)(2,1)}), bf16[128,3,320]{2,1,0:T(4,128)(2,1)S(1)}, u32[]{:S(2)}, u32[]{:S(2)}) %all-to-all-start.1) | async-done | bytes 245792 | tf_op jit(solution)/shard_map/all_to_all | solution.py:173
  170.0 0.7 copy.191
  170.7 3.5 all-to-all-start.4
  174.4 5.0 %all-to-all-done.4 = bf16[4,3,64,128]{3,2,1,0:T(8,128)(2,1)S(1)} async-done(((bf16[4,3,64,128]{3,2,1,0:T(8,128)(2,1)}), bf16[4,3,64,128]{3,2,1,0:T(8,128)(2,1)S(1)}, u32[]{:S(2)}, u32[]{:S(2)}) %all-to-all-start.4) | async-done | bytes 196640 | tf_op jit(solution)/shard_map/all_to_all | solution.py:192
  179.4 3.6 fusion.9
  183.0 1.2 convert_reduce_fusion.1
  184.4 0.7 copy.196
  185.0 0.7 copy.197
  185.7 3.5 fusion.5
  189.2 1.1 pad_maximum_fusion
  190.3 3.5 all-to-all-start.5
  193.7 0.8 select_reduce_fusion
  194.8 6.3 %all-to-all-done.5 = bf16[4,3,8,8,130]{4,3,2,1,0:T(8,128)(2,1)S(1)} async-done(((bf16[4,3,8,8,130]{4,3,2,1,0:T(8,128)(2,1)}), bf16[4,3,8,8,130]{4,3,2,1,0:T(8,128)(2,1)S(1)}, u32[]{:S(2)}, u32[]{:S(2)}) %all-to-all-start.5) | async-done | bytes 199712 | tf_op jit(solution)/shard_map/all_to_all | solution.py:48
  201.3 0.6 copy.245
  201.9 0.6 copy.249
  203.3 6.5 %copy.240 = bf16[4,3,8,8,128]{0,1,4,3,2:T(4,128)(2,1)} copy(bf16[4,3,8,8,128]{4,3,1,2,0:T(8,128)(2,1)S(1)} %fusion.18) | data formatting | bytes 393216 | tf_op jit(solution)/shard_map/convert_element_type | solution.py:129
  209.8 12.6 %reshape.321 = bf16[32,2,1536]{2,1,0:T(2,128)(2,1)S(1)} reshape(bf16[8192,3,4]{2,1,0:T(4,128)(2,1)} %bitcast.156) | data formatting | bytes 393216
  222.4 14.6 %all_to_all.67 = bf16[32,2,1536]{2,1,0:T(2,128)(2,1)S(1)} all-to-all(bf16[32,2,1536]{2,1,0:T(2,128)(2,1)S(1)} %reshape.321), channel_id=1, replica_groups=mesh['group_0'=2,'group_1'=2,'tensor'=32] {'tensor'}, dimensions={0} | all-to-all | bytes 393216 | tf_op jit(solution)/shard_map/all_to_all | solution.py:215
  236.9 10.4 %reshape.322 = bf16[8192,3,4]{2,1,0:T(4,128)(2,1)} reshape(bf16[32,2,1536]{2,1,0:T(2,128)(2,1)S(1)} %all_to_all.67) | data formatting | bytes 393216
  247.3 7.9 %copy.241 = bf16[4,3,32,256]{3,2,0,1:T(8,128)(2,1)S(1)} copy(bf16[4,3,32,256]{0,1,3,2:T(4,128)(2,1)} %bitcast.157) | data formatting | bytes 393216 | tf_op jit(solution)/shard_map/all_to_all | solution.py:215
  255.4 6.7 %convolution_convert_fusion = bf16[128,3,8192]{2,0,1:T(8,128)(2,1)} fusion(bf16[128,3,256]{2,0,1:T(8,128)(2,1)S(1)} %all_to_all.56, bf16[256,8192]{1,0:T(8,128)(2,1)} %param.11), kind=kOutput, calls=%fused_computation.3 | convolution fusion | flops 1613758464 | bytes 10682368 | tf_op jit(solution)/shard_map/rsc,cd->rsd/dot_general | solution.py:217
  262.1 10.2 %reshape.292 = bf16[32,4,3,8192]{3,1,0,2:T(4,128)(2,1)} reshape(bf16[128,3,8192]{2,0,1:T(8,128)(2,1)} %convolution_convert_fusion) | data formatting | bytes 12582912 | tf_op jit(solution)/shard_map/reshape | solution.py:21
  272.3 5.7 %copy.221 = bf16[32,4,3,8192]{3,1,2,0:T(4,128)(2,1)S(1)} copy(bf16[32,4,3,8192]{3,1,0,2:T(4,128)(2,1)} %reshape.292) | data formatting | bytes 12582912 | tf_op jit(solution)/shard_map/reshape | solution.py:21
  277.9 77.5 %all_to_all.68 = bf16[32,4,3,8192]{3,1,2,0:T(4,128)(2,1)S(1)} all-to-all(bf16[32,4,3,8192]{3,1,2,0:T(4,128)(2,1)S(1)} %copy.221), channel_id=1, replica_groups=mesh['group_0'=2,'group_1'=2,'tensor'=32] {'tensor'}, dimensions={0} | all-to-all | bytes 12582912 | tf_op jit(solution)/shard_map/all_to_all | solution.py:61
  355.4 3.0 convert_reduce_fusion
  358.5 0.8 fusion.23
  (51 shorter events, 4.1 us)
Async XLA Ops:
  0.0 31.8 %copy-start = (s32[1,12]{1,0:T(1,128)S(1)}, s32[1,12]{1,0:T(1,128)}, u32[]{:S(2)}) copy-start(s32[1,12]{1,0:T(1,128)} %param.14) | copy-start | bytes 148
  4.4 6.9 %all-to-all-start.2 = ((s32[2,2,1]{1,2,0:T(1,128)}), s32[2,2,1]{1,2,0:T(1,128)S(1)}, u32[]{:S(2)}, u32[]{:S(2)}) async-start(s32[2,2,1]{1,2,0:T(1,128)} %bitcast.15), calls=%async_computation.2 | async-start | bytes 2048 | tf_op jit(solution)/shard_map/all_to_all | solution.py:35
  20.7 101.5 %all-to-all-start = ((bf16[32,4,3,8192]{3,1,2,0:T(4,128)(2,1)}), bf16[32,4,3,8192]{3,1,2,0:T(4,128)(2,1)}, u32[]{:S(2)}, u32[]{:S(2)}) async-start(bf16[32,4,3,8192]{3,1,2,0:T(4,128)(2,1)} %stack.2), calls=%async_computation | async-start | bytes 12582912 | tf_op jit(solution)/shard_map/all_to_all | solution.py:169
  150.8 18.0 %all-to-all-start.1 = ((bf16[128,3,320]{2,1,0:T(4,128)(2,1)}), bf16[128,3,320]{2,1,0:T(4,128)(2,1)S(1)}, u32[]{:S(2)}, u32[]{:S(2)}) async-start(bf16[128,3,320]{2,1,0:T(4,128)(2,1)} %copy.183), calls=%async_computation.1 | async-start | bytes 786432 | tf_op jit(solution)/shard_map/all_to_all | solution.py:173
  170.7 8.7 %all-to-all-start.4 = ((bf16[4,3,64,128]{3,2,1,0:T(8,128)(2,1)}), bf16[4,3,64,128]{3,2,1,0:T(8,128)(2,1)S(1)}, u32[]{:S(2)}, u32[]{:S(2)}) async-start(bf16[4,3,64,128]{3,2,1,0:T(8,128)(2,1)} %copy.191), calls=%async_computation.4 | async-start | bytes 393216 | tf_op jit(solution)/shard_map/all_to_all | solution.py:192
  190.3 10.9 %all-to-all-start.5 = ((bf16[4,3,8,8,130]{4,3,2,1,0:T(8,128)(2,1)}), bf16[4,3,8,8,130]{4,3,2,1,0:T(8,128)(2,1)S(1)}, u32[]{:S(2)}, u32[]{:S(2)}) async-start(bf16[4,3,8,8,130]{4,3,2,1,0:T(8,128)(2,1)} %pad_maximum_fusion), calls=%async_computation.5 | async-start | bytes 786432 | tf_op jit(solution)/shard_map/all_to_all | solution.py:48
  277.9 81.3 %copy-start.1 = (s32[1,12]{1,0:T(1,128)S(1)}, s32[1,12]{1,0:T(1,128)}, u32[]{:S(2)}) copy-start(s32[1,12]{1,0:T(1,128)} %param.14) | copy-start | bytes 148
  355.4 3.0 copy-start.2
